TPU v7x, 512 devices: a whole 4x8x8 slice. The times are simulated.
512 devices in a mesh: trow: 8 (over y), tcol: 8 (over x, z_lo), dp: 8 (over z_hi, core).
Axes of the slice: x: 4, y: 8, z: 8 (z_hi: 4, z_lo: 2; z = z_hi * 2 + z_lo), core: 2. Of those that a mesh axis runs over, the one named last changes fastest.
Arguments:
- embeds: bfloat16 [8192, 1024], P('dp'), may hold values from -6 to 6
- frequencies: bfloat16 [1024, 8192], P(None, ('trow', 'tcol')), may hold values from -0.5 to 0.5
- phases: float32 [8192], P(('trow', 'tcol')), may hold values from -3.140625 to 3.140625
- labels: int32 [8192], P('dp'), may hold values from 0 to 999
- weights: float32 [8192, 1000], P(('tcol', 'dp'), 'trow'), may hold values from -6 to 6
Outputs:
- gram_matrix: float32 [8192, 8192], P(('trow', 'dp'), 'tcol')
- new_weights: float32 [8192, 1000], P(('tcol', 'dp'), 'trow')
All inputs are finite; a program needn't handle non-finite values.
Results may differ from a plain program's by a relative error of at most 0.023.
Values may be sent and summed in bfloat16 or wider, within the bound.
A program may use at most 64 MiB of HBM per device.

v0:
```python
import jax
import jax.numpy as jnp
from jax import lax
from jax.sharding import PartitionSpec as P

C = 1000
ROOT_TWO = 1.4142135623730951
RIDGE = 0.5
STEP_RATE = 0.5


def copy_for_each(array, axis):
    size = lax.axis_size(axis)
    return lax.all_to_all(
        jnp.broadcast_to(array[None], (size, *array.shape)), axis, 0, 0, tiled=True
    )


def laid_out(parts, dim):
    dims = list(parts.shape[1:])
    dims[dim] *= parts.shape[0]
    return jnp.moveaxis(parts, 0, dim).reshape(dims)


def gather_directly(array, axis, dim):
    parts = copy_for_each(array, axis)
    return laid_out(parts, dim)


def padded_to(lines, size):
    spare = -lines.shape[0] % size
    if not spare:
        return lines
    return jnp.concatenate([lines, jnp.zeros((spare, *lines.shape[1:]), lines.dtype)])


def broadcast_by_parts(array, axis, root):
    lines = jnp.where(lax.axis_index(axis) == root, array, jnp.zeros_like(array)).reshape(
        -1, *array.shape[1:][-1:]
    )
    padded = padded_to(lines, lax.axis_size(axis))
    own = lax.psum_scatter(padded, axis, scatter_dimension=0, tiled=True)
    return lax.all_gather(own, axis, axis=0, tiled=True)[: len(lines)].reshape(array.shape)


def split_up(array, dim, size):
    dims = array.shape
    parts = array.reshape(*dims[:dim], size, dims[dim] // size, *dims[dim + 1 :])
    return jnp.moveaxis(parts, dim, 0)


def sum_at_owner(array, axis, dim):
    parts = split_up(array, dim, lax.axis_size(axis))
    arrived = lax.all_to_all(parts, axis, split_axis=0, concat_axis=0, tiled=True)
    return arrived.astype(jnp.float32).sum(axis=0)


def of_everyone(array, axis):
    everything = copy_for_each(array, axis)
    return jnp.sum(everything.astype(jnp.float32), axis=0)


def broadcast(array, axis, root):
    return lax.dynamic_index_in_dim(lax.all_gather(array, axis), root, 0, keepdims=False)


def featurize(embeds, frequencies, phases):
    angles = jnp.dot(embeds, frequencies, preferred_element_type=jnp.float32) + phases
    return (ROOT_TWO * jnp.cos(angles)).astype(jnp.bfloat16)


def shards(embeds, frequencies, phases, labels, weights):
    rows_here = embeds.shape[0]
    n_row = lax.axis_size("trow")
    n_dp = lax.axis_size("dp")
    row_idx = lax.axis_index("trow")
    col_idx = lax.axis_index("tcol")
    dp_idx = lax.axis_index("dp")
    total_rows = rows_here * n_dp
    contract = (((0,), (0,)), ((), ()))
    own_part = featurize(embeds, frequencies, phases)
    left_feats = gather_directly(own_part, "tcol", 1)
    right_feats = broadcast_by_parts(left_feats, "trow", col_idx)
    tile_width = left_feats.shape[1]
    sub_rows = tile_width // n_dp
    gram_part = lax.psum_scatter(
        (
            lax.dot_general(left_feats, right_feats, contract, preferred_element_type=jnp.float32)
            / total_rows
        ).astype(jnp.bfloat16),
        "dp",
        scatter_dimension=0,
        tiled=True,
    ).astype(jnp.float32)
    global_rows = row_idx * tile_width + dp_idx * sub_rows + jnp.arange(sub_rows, dtype=jnp.int32)
    global_cols = col_idx * tile_width + jnp.arange(tile_width, dtype=jnp.int32)
    gram_rows = gram_part + RIDGE * (global_rows[:, None] == global_cols[None, :]).astype(
        jnp.float32
    )
    class_width = weights.shape[1]
    class_ids = row_idx * class_width + jnp.arange(class_width, dtype=jnp.int32)
    onehot = (labels[:, None] == class_ids[None, :]).astype(jnp.bfloat16)
    label_term = lax.dot_general(
        right_feats, onehot, contract, preferred_element_type=jnp.float32
    ) * (C / total_rows)
    label_rows = sum_at_owner(label_term.astype(jnp.bfloat16), "dp", 0)
    gram_three = gram_rows.astype(jnp.bfloat16).reshape(sub_rows, n_dp, sub_rows)
    block_ids = jnp.arange(n_row, dtype=jnp.int32)
    local_weights = weights.astype(jnp.bfloat16)[None]
    pieces = lax.all_gather(local_weights, ("trow", "dp"), axis=0, tiled=True)
    positions = jnp.arange(pieces.shape[0], dtype=jnp.int32)
    sub_index = positions % n_dp
    owner_index = positions // n_dp
    chosen = jnp.take(gram_three, sub_index, axis=1)
    products = jnp.einsum("rpk,pkc->rpc", chosen, pieces, preferred_element_type=jnp.float32)
    placing = (owner_index[:, None] == block_ids[None, :]).astype(jnp.float32)
    folded = jnp.einsum("rpc,pi->ric", products, placing)
    curv_local = folded.reshape(sub_rows, n_row * class_width)
    diag_block = lax.dynamic_slice_in_dim(gram_rows, dp_idx * sub_rows, sub_rows, 1)
    diag_local = jnp.diagonal(diag_block) * (row_idx == col_idx).astype(jnp.float32)
    row_total = of_everyone(curv_local.astype(jnp.bfloat16), "tcol").astype(jnp.float32)
    received, diag_vals = (
        broadcast(row_total.astype(jnp.bfloat16), "trow", col_idx).astype(row_total.dtype),
        broadcast(diag_local.astype(jnp.bfloat16), "trow", col_idx).astype(diag_local.dtype),
    )
    curv_mine = lax.dynamic_slice_in_dim(received, row_idx * class_width, class_width, 1)
    updated = weights - STEP_RATE * (curv_mine - label_rows) / diag_vals[:, None]
    return (gram_rows, updated)


def solution(mesh):
    return jax.shard_map(
        shards,
        mesh=mesh,
        in_specs=(
            P("dp", None),
            P(None, ("trow", "tcol")),
            P(("trow", "tcol")),
            P("dp"),
            P(("tcol", "dp"), "trow"),
        ),
        out_specs=(P(("trow", "dp"), "tcol"), P(("tcol", "dp"), "trow")),
        check_vma=False,
    )
```

profile of v0, /device:TPU:16, one launch (start us, length us, event | category | flops | bytes accessed | tf_op | source)
XLA Modules:
  0.0 348.0 jit_solution(17416006484841058802)
XLA Ops:
  8.0 0.0 copy-start
  8.0 1.6 copy-done
  9.6 3.3 fusion.5
  12.9 0.1 copy.15
  13.1 1.6 broadcast_in_dim.20
  14.7 6.1 %all-to-all-start = ((bf16[8,1024,128]{1,2,0:T(8,128)(2,1)}), bf16[8,1024,128]{1,2,0:T(8,128)(2,1)}, u32[]{:S(2)}, u32[]{:S(2)}) async-start(bf16[8,1024,128]{1,2,0:T(8,128)(2,1)} %broadcast_in_dim.20), calls=%async_computation | async-start | bytes 4194304 | tf_op jit(solution)/shard_map/all_to_all | solution.py:14
  20.8 0.0 reduce-scatter.7.cloned.1.call-start
  20.9 27.0 %all-to-all-done = bf16[8,1024,128]{1,2,0:T(8,128)(2,1)} async-done(((bf16[8,1024,128]{1,2,0:T(8,128)(2,1)}), bf16[8,1024,128]{1,2,0:T(8,128)(2,1)}, u32[]{:S(2)}, u32[]{:S(2)}) %all-to-all-start) | async-done | bytes 2097184 | tf_op jit(solution)/shard_map/all_to_all | solution.py:14
  47.9 3.0 broadcast_select_fusion
  50.9 3.9 %copy.20 = bf16[1024,1024]{1,0:T(8,128)(2,1)} copy(bf16[1024,1024]{0,1:T(8,128)(2,1)} %broadcast_select_fusion) | data formatting | bytes 4194304
  54.9 0.0 reduce-scatter.7.cloned.1.call-update
  54.9 0.0 all-gather.8.cloned.1.call-start
  55.0 45.5 %reduce-scatter.7.cloned.1.call-done = bf16[128,1024]{1,0:T(8,128)(2,1)} async-done(((bf16[1024,1024]{1,0:T(8,128)(2,1)}), bf16[128,1024]{1,0:T(8,128)(2,1)}) %reduce-scatter.7.cloned.1.call-update) | async-done | bytes 262160
  100.5 1.8 copy.21
  102.3 0.0 all-gather.8.cloned.1.call-update
  102.3 0.0 reduce-scatter.5.cloned.1.call-start
  102.4 51.8 %all-gather.8.cloned.1.call-done = bf16[1024,1024]{0,1:T(8,128)(2,1)} async-done(((bf16[128,1024]{0,1:T(8,128)(2,1)}), bf16[1024,1024]{0,1:T(8,128)(2,1)}) %all-gather.8.cloned.1.call-update) | async-done | bytes 2097168 | tf_op jit(solution)/shard_map/all_gather | solution.py:43
  154.2 5.9 %multiply_convert_fusion = bf16[1024,1024]{1,0:T(8,128)(2,1)} fusion(bf16[1024,1024]{0,1:T(8,128)(2,1)} %bitcast.1, bf16[1024,1024]{0,1:T(8,128)(2,1)} %all-gather.8.cloned.1.call-done), kind=kOutput, calls=%fused_computation.2 | convolution fusion | flops 2149580800 | bytes 6291456 | tf_op jit(solution)/shard_map/dot_general | solution.py:88
  160.1 0.0 reduce-scatter.5.cloned.1.call-update
  160.1 0.0 all-gather.10.cloned.1.call-start
  160.2 0.8 copy-done.2
  160.9 0.6 convert_element_type.73
  161.6 0.0 all-gather.10.cloned.1.call-update
  161.6 0.0 all-gather.12.cloned.1.call-start
  161.7 44.9 %reduce-scatter.5.cloned.1.call-done = bf16[128,1024]{1,0:T(8,128)(2,1)} async-done(((bf16[1024,1024]{1,0:T(8,128)(2,1)}), bf16[128,1024]{1,0:T(8,128)(2,1)}) %reduce-scatter.5.cloned.1.call-update) | async-done | bytes 262160 | tf_op jit(solution)/shard_map/reduce_scatter | solution.py:86
  206.6 1.1 convert_bitcast_fusion
  207.7 0.0 copy-start.1
  207.8 2.1 gather_fusion
  209.9 38.0 %all-gather.10.cloned.1.call-done = bf16[8192,125]{1,0:T(8,128)(2,1)} async-done(((bf16[128,125]{1,0:T(8,128)(2,1)}), bf16[8192,125]{1,0:T(8,128)(2,1)}) %all-gather.10.cloned.1.call-update) | async-done | bytes 2048016 | tf_op jit(solution)/shard_map/all_gather | solution.py:110
  247.9 4.3 %convolution_bitcast_fusion = bf16[128,64,125]{2,0,1:T(8,128)(2,1)} fusion(bf16[64,128,125]{2,1,0:T(8,128)(2,1)} %bitcast.56, bf16[64,128,128]{2,1,0:T(8,128)(2,1)} %gather_fusion, pred[64]{0:T(512)(128)(4,1)S(1)} %compare_and_fusion), kind=kOutput, calls=%fused_computation.3 | convolution fusion | flops 263192576 | bytes 6193216 | tf_op jit(solution)/shard_map/rpk,pkc->rpc/dot_general | solution.py:115
  252.2 4.1 %copy.17 = bf16[128,64,125]{0,1,2:T(8,128)(2,1)} copy(bf16[128,64,125]{2,0,1:T(8,128)(2,1)} %convolution_bitcast_fusion) | data formatting | bytes 4096000 | tf_op jit(solution)/shard_map/rpk,pkc->rpc/transpose | solution.py:115
  256.3 1.9 fusion.7
  258.3 0.1 convert_element_type.76
  258.4 0.3 broadcast_in_dim.27
  258.7 31.2 %all_to_all.15 = bf16[8,128,1000]{1,2,0:T(8,128)(2,1)} all-to-all(bf16[8,128,1000]{1,2,0:T(8,128)(2,1)S(1)} %broadcast_in_dim.27), channel_id=1, replica_groups=mesh['trow'=8,'tcol'=8,'dp'=8] {'tcol'}, dimensions={0} | all-to-all | bytes 4096000 | tf_op jit(solution)/shard_map/all_to_all | solution.py:14
  289.9 2.6 reduce_sum.21
  292.5 0.0 all-gather.12.cloned.1.call-update
  292.6 3.1 fusion.6
  295.7 3.9 %all-to-all-start.2 = ((bf16[8,128,125]{2,1,0:T(8,128)(2,1)}), bf16[8,128,125]{2,1,0:T(8,128)(2,1)S(1)}, u32[]{:S(2)}, u32[]{:S(2)}) async-start(bf16[8,128,125]{2,1,0:T(8,128)(2,1)} %bitcast.10), calls=%async_computation.3 | async-start | bytes 524288 | tf_op jit(solution)/shard_map/all_to_all | solution.py:54
  299.6 12.3 %all-to-all-done.2 = bf16[8,128,125]{2,1,0:T(8,128)(2,1)S(1)} async-done(((bf16[8,128,125]{2,1,0:T(8,128)(2,1)}), bf16[8,128,125]{2,1,0:T(8,128)(2,1)S(1)}, u32[]{:S(2)}, u32[]{:S(2)}) %all-to-all-start.2) | async-done | bytes 256032 | tf_op jit(solution)/shard_map/all_to_all | solution.py:54
  311.9 0.1 convert_reduce_fusion
  312.0 1.2 gather_fusion.1
  313.3 12.9 %all-gather.3 = bf16[8,1,128]{2,1,0:T(2,128)(2,1)S(1)} all-gather(bf16[1,1,128]{2,1,0:T(2,128)(2,1)S(1)} %convert_bitcast_fusion.1), channel_id=4, replica_groups=mesh['trow'=8,'tcol'=8,'dp'=8] {'trow'}, dimensions={0}, use_global_device_ids=true | all-gather | bytes 2304 | tf_op jit(solution)/shard_map/all_gather | solution.py:64
  326.1 11.7 %all-gather.12.cloned.1.call-done = bf16[1024,1000]{0,1:T(8,128)(2,1)} async-done(((bf16[128,1000]{0,1:T(8,128)(2,1)}), bf16[1024,1000]{0,1:T(8,128)(2,1)}) %all-gather.12.cloned.1.call-update) | async-done | bytes 2048016 | tf_op jit(solution)/shard_map/all_gather | solution.py:64
  337.8 2.2 copy.23
  340.0 0.1 dynamic-slice_convert_fusion
  340.1 0.1 copy.19
  340.2 0.7 fusion.14
  (17 shorter events, 0.2 us)
Async XLA Ops:
  8.0 1.6 copy-start
  14.7 33.2 %all-to-all-start = ((bf16[8,1024,128]{1,2,0:T(8,128)(2,1)}), bf16[8,1024,128]{1,2,0:T(8,128)(2,1)}, u32[]{:S(2)}, u32[]{:S(2)}) async-start(bf16[8,1024,128]{1,2,0:T(8,128)(2,1)} %broadcast_in_dim.20), calls=%async_computation | async-start | bytes 4194304 | tf_op jit(solution)/shard_map/all_to_all | solution.py:14
  20.8 79.7 %reduce-scatter.7.cloned.1.call-start = ((), (), s32[]{:S(2)}) async-start(), calls=%async_computation.9 | async-start | bytes 2359296
  54.9 99.3 %all-gather.8.cloned.1.call-start = ((), (), s32[]{:S(2)}) async-start(), calls=%async_computation.5 | async-start | bytes 2359296 | tf_op jit(solution)/shard_map/all_gather | solution.py:43
  102.3 104.3 %reduce-scatter.5.cloned.1.call-start = ((), (), s32[]{:S(2)}) async-start(), calls=%async_computation.6 | async-start | bytes 2359296 | tf_op jit(solution)/shard_map/reduce_scatter | solution.py:86
  160.1 0.8 copy-start.2
  160.1 87.8 %all-gather.10.cloned.1.call-start = ((), (), s32[]{:S(2)}) async-start(), calls=%async_computation.7 | async-start | bytes 2129920 | tf_op jit(solution)/shard_map/all_gather | solution.py:110
  161.6 176.2 %all-gather.12.cloned.1.call-start = ((), (), s32[]{:S(2)}) async-start(), calls=%async_computation.8 | async-start | bytes 2304000 | tf_op jit(solution)/shard_map/all_gather | solution.py:64
  207.7 104.3 %copy-start.1 = (f32[128,1024]{1,0:T(8,128)}, f32[128,1024]{1,0:T(8,128)S(1)}, u32[]{:S(2)}) copy-start(f32[128,1024]{1,0:T(8,128)S(1)} %get-tuple-element.3) | copy-start | bytes 1572868
  289.9 2.7 copy-start.3
  295.7 16.2 %all-to-all-start.2 = ((bf16[8,128,125]{2,1,0:T(8,128)(2,1)}), bf16[8,128,125]{2,1,0:T(8,128)(2,1)S(1)}, u32[]{:S(2)}, u32[]{:S(2)}) async-start(bf16[8,128,125]{2,1,0:T(8,128)(2,1)} %bitcast.10), calls=%async_computation.3 | async-start | bytes 524288 | tf_op jit(solution)/shard_map/all_to_all | solution.py:54
Sparse Core Ops, SparseCore 0:
  55.0 45.4 reduce-scatter.6
  103.1 51.0 all-gather.7
  160.2 46.2 reduce-scatter.4
  292.7 45.1 all-gather.11
Sparse Core Ops, SparseCore 1:
  164.5 83.4 all-gather.9
where the time goes:
time: 349 us; the launch traced here: 348 us
  waiting for transfers between devices  231 us (66%)
  blocking collectives  44.1 us (13%)
  local copies, waits for them, and re-layouts  20.1 us (6%)
  matrix products  18.6 us (5%)
  between operations  15.4 us (4%)
  starting transfers between devices  10.2 us (3%)
  other arithmetic  8.31 us (2%)
    all_gather x1, waiting for transfers between devices, broadcast_by_parts(): lax.all_gather(own, axis, axis=0, tiled=True)[:len(lines)]  51.8 us
    unnamed x6, waiting for transfers between devices  45.6 us
    reduce_scatter x1, waiting for transfers between devices, shards(): lax.psum_scatter((lax.dot_general(left_feats, right_feats, contract, pref...  44.9 us
    all_gather x1, waiting for transfers between devices, shards(): pieces = lax.all_gather(local_weights, ('trow', 'dp'), axis=0, tiled=True)  38 us
    all_to_all x1, blocking collectives, copy_for_each(): lax.all_to_all(jnp.broadcast_to(array[None], (size, *array.shape)), axis,...  31.2 us
    all_to_all x1, waiting for transfers between devices, copy_for_each(): lax.all_to_all(jnp.broadcast_to(array[None], (size, *array.shape)), axis,...  27 us
    all_gather x1, blocking collectives, broadcast(): lax.all_gather(array, axis)  12.9 us
    all_to_all x1, waiting for transfers between devices, sum_at_owner(): lax.all_to_all(parts, axis, split_axis=0, concat_axis=0, tiled=True)  12.3 us
  transfers between devices with their start and end apart: 7, of which 7 were waited for; matrix products, arithmetic and copies ran while one was open for 2% of the time, Pallas kernels for 0%

commit v1 on v0

--- a/solution.py
+++ b/solution.py
@@ -7,6 +7,12 @@
 ROOT_TWO = 1.4142135623730951
 RIDGE = 0.5
 STEP_RATE = 0.5
+
+
+def divide_the_side(w_in, mesh_name, on_dim):
+    y = jnp.stack([w_in for _ in range(jax.lax.axis_size(mesh_name))])
+    o_now = jax.lax.all_to_all(y, axis_name=mesh_name, split_axis=0, concat_axis=0)
+    return jnp.concatenate(o_now, axis=on_dim)
 
 
 def copy_for_each(array, axis):
@@ -40,7 +46,7 @@
     )
     padded = padded_to(lines, lax.axis_size(axis))
     own = lax.psum_scatter(padded, axis, scatter_dimension=0, tiled=True)
-    return lax.all_gather(own, axis, axis=0, tiled=True)[: len(lines)].reshape(array.shape)
+    return divide_the_side(own, mesh_name=axis, on_dim=0)[: len(lines)].reshape(array.shape)
 
 
 def split_up(array, dim, size):

time: 349 us -> 348 us (level)
  waiting for transfers between devices: 231 us -> 180 us
  blocking collectives: 44.1 us -> 94.9 us
    all_gather x1 -> x0, waiting for transfers between devices: 51.8 us -> none  [broadcast_by_parts(): lax.all_gather(own, axis, axis=0, tiled=True)[:len(lines)]]
    all_to_all x0 -> x1, blocking collectives: none -> 50.9 us  [divide_the_side(): jax.lax.all_to_all(y, axis_name=mesh_name, split_axis=0, concat_axis=0)]
    unnamed x6 -> x4, waiting for transfers between devices: 45.6 us -> 0.07 us
    reduce_scatter x0 -> x1, waiting for transfers between devices: none -> 45.5 us  [broadcast_by_parts(): own = lax.psum_scatter(padded, axis, scatter_dimension=0, tiled=True)]
    unnamed x11 -> x12, local copies, waits for them, and re-layouts: 10.3 us -> 9.81 us
  transfers between devices with their start and end apart: 7 -> 6, of which waited for: 7 -> 6; matrix products, arithmetic and copies ran while one was open for 2% -> 2% of each run, Pallas kernels for 0% -> 0%
where the time goes in v1:
time: 348 us; the launch traced here: 347 us
  waiting for transfers between devices  180 us (52%)
  blocking collectives  94.9 us (27%)
  local copies, waits for them, and re-layouts  20.8 us (6%)
  matrix products  18.1 us (5%)
  between operations  15.4 us (4%)
  starting transfers between devices  10.2 us (3%)
  other arithmetic  8.31 us (2%)
    all_to_all x1, blocking collectives, divide_the_side(): jax.lax.all_to_all(y, axis_name=mesh_name, split_axis=0, concat_axis=0)  50.9 us
    reduce_scatter x1, waiting for transfers between devices, broadcast_by_parts(): own = lax.psum_scatter(padded, axis, scatter_dimension=0, tiled=True)  45.5 us
    reduce_scatter x1, waiting for transfers between devices, shards(): lax.psum_scatter((lax.dot_general(left_feats, right_feats, contract, pref...  45.1 us
    all_gather x1, waiting for transfers between devices, shards(): pieces = lax.all_gather(local_weights, ('trow', 'dp'), axis=0, tiled=True)  38.1 us
    all_to_all x1, blocking collectives, copy_for_each(): lax.all_to_all(jnp.broadcast_to(array[None], (size, *array.shape)), axis,...  31.2 us
    all_to_all x1, waiting for transfers between devices, copy_for_each(): lax.all_to_all(jnp.broadcast_to(array[None], (size, *array.shape)), axis,...  27 us
    all_gather x1, blocking collectives, broadcast(): lax.all_gather(array, axis)  12.9 us
    all_to_all x1, waiting for transfers between devices, sum_at_owner(): lax.all_to_all(parts, axis, split_axis=0, concat_axis=0, tiled=True)  12.3 us
  transfers between devices with their start and end apart: 6, of which 6 were waited for; matrix products, arithmetic and copies ran while one was open for 2% of the time, Pallas kernels for 0%

profile of v1, /device:TPU:16, one launch (start us, length us, event | category | flops | bytes accessed | tf_op | source)
XLA Modules:
  0.0 347.4 jit_solution(7969147184682010999)
XLA Ops:
  8.0 0.0 copy-start
  8.0 1.6 copy-done
  9.6 3.3 fusion.5
  12.9 0.1 copy.17
  13.1 1.6 broadcast_in_dim.20
  14.7 6.1 %all-to-all-start = ((bf16[8,1024,128]{1,2,0:T(8,128)(2,1)}), bf16[8,1024,128]{1,2,0:T(8,128)(2,1)}, u32[]{:S(2)}, u32[]{:S(2)}) async-start(bf16[8,1024,128]{1,2,0:T(8,128)(2,1)} %broadcast_in_dim.20), calls=%async_computation | async-start | bytes 4194304 | tf_op jit(solution)/shard_map/all_to_all | solution.py:20
  20.8 0.0 reduce-scatter.7.cloned.1.call-start
  20.9 27.0 %all-to-all-done = bf16[8,1024,128]{1,2,0:T(8,128)(2,1)} async-done(((bf16[8,1024,128]{1,2,0:T(8,128)(2,1)}), bf16[8,1024,128]{1,2,0:T(8,128)(2,1)}, u32[]{:S(2)}, u32[]{:S(2)}) %all-to-all-start) | async-done | bytes 2097184 | tf_op jit(solution)/shard_map/all_to_all | solution.py:20
  47.9 3.1 broadcast_select_fusion
  51.0 3.9 %copy.23 = bf16[1024,1024]{1,0:T(8,128)(2,1)} copy(bf16[1024,1024]{0,1:T(8,128)(2,1)} %broadcast_select_fusion) | data formatting | bytes 4194304
  54.9 0.0 reduce-scatter.7.cloned.1.call-update
  54.9 0.0 reduce-scatter.5.cloned.1.call-start
  55.0 45.5 %reduce-scatter.7.cloned.1.call-done = bf16[128,1024]{1,0:T(8,128)(2,1)} async-done(((bf16[1024,1024]{1,0:T(8,128)(2,1)}), bf16[128,1024]{1,0:T(8,128)(2,1)}) %reduce-scatter.7.cloned.1.call-update) | async-done | bytes 262160 | tf_op jit(solution)/shard_map/reduce_scatter | solution.py:48
  100.5 1.2 stack.2
  101.7 50.9 %all_to_all.20 = bf16[8,128,1024]{2,1,0:T(8,128)(2,1)S(1)} all-to-all(bf16[8,128,1024]{2,1,0:T(8,128)(2,1)S(1)} %stack.2), channel_id=1, replica_groups=mesh['trow'=8,'tcol'=8,'dp'=8] {'trow'}, dimensions={0} | all-to-all | bytes 4194304 | tf_op jit(solution)/shard_map/all_to_all | solution.py:14
  152.6 1.3 copy-done.1
  153.9 5.3 %multiply_convert_fusion = bf16[1024,1024]{1,0:T(8,128)(2,1)} fusion(bf16[1024,1024]{0,1:T(8,128)(2,1)} %bitcast.1, bf16[1024,1024]{1,0:T(8,128)(2,1)S(1)} %bitcast.58), kind=kOutput, calls=%fused_computation.2 | convolution fusion | flops 2149580800 | bytes 6291456 | tf_op jit(solution)/shard_map/dot_general | solution.py:94
  159.2 0.0 reduce-scatter.5.cloned.1.call-update
  159.2 0.0 all-gather.7.cloned.1.call-start
  159.3 0.8 copy-done.3
  160.0 0.6 convert_element_type.73
  160.6 0.0 all-gather.7.cloned.1.call-update
  160.7 0.0 all-gather.9.cloned.1.call-start
  160.8 45.1 %reduce-scatter.5.cloned.1.call-done = bf16[128,1024]{1,0:T(8,128)(2,1)} async-done(((bf16[1024,1024]{1,0:T(8,128)(2,1)}), bf16[128,1024]{1,0:T(8,128)(2,1)}) %reduce-scatter.5.cloned.1.call-update) | async-done | bytes 262160 | tf_op jit(solution)/shard_map/reduce_scatter | solution.py:92
  205.9 1.1 convert_bitcast_fusion
  207.0 0.0 copy-start.2
  207.0 2.2 gather_fusion
  209.2 38.1 %all-gather.7.cloned.1.call-done = bf16[8192,125]{1,0:T(8,128)(2,1)} async-done(((bf16[128,125]{1,0:T(8,128)(2,1)}), bf16[8192,125]{1,0:T(8,128)(2,1)}) %all-gather.7.cloned.1.call-update) | async-done | bytes 2048016 | tf_op jit(solution)/shard_map/all_gather | solution.py:116
  247.3 4.3 %convolution_bitcast_fusion = bf16[128,64,125]{2,0,1:T(8,128)(2,1)} fusion(bf16[64,128,125]{2,1,0:T(8,128)(2,1)} %bitcast.57, bf16[64,128,128]{2,1,0:T(8,128)(2,1)} %gather_fusion, pred[64]{0:T(512)(128)(4,1)S(1)} %compare_and_fusion), kind=kOutput, calls=%fused_computation.3 | convolution fusion | flops 263192576 | bytes 6193216 | tf_op jit(solution)/shard_map/rpk,pkc->rpc/dot_general | solution.py:121
  251.6 4.1 %copy.20 = bf16[128,64,125]{0,1,2:T(8,128)(2,1)} copy(bf16[128,64,125]{2,0,1:T(8,128)(2,1)} %convolution_bitcast_fusion) | data formatting | bytes 4096000 | tf_op jit(solution)/shard_map/rpk,pkc->rpc/transpose | solution.py:121
  255.7 1.9 fusion.7
  257.7 0.1 convert_element_type.76
  257.8 0.3 broadcast_in_dim.27
  258.0 31.2 %all_to_all.21 = bf16[8,128,1000]{1,2,0:T(8,128)(2,1)} all-to-all(bf16[8,128,1000]{1,2,0:T(8,128)(2,1)S(1)} %broadcast_in_dim.27), channel_id=1, replica_groups=mesh['trow'=8,'tcol'=8,'dp'=8] {'tcol'}, dimensions={0} | all-to-all | bytes 4096000 | tf_op jit(solution)/shard_map/all_to_all | solution.py:20
  289.2 2.6 reduce_sum.21
  291.9 0.0 all-gather.9.cloned.1.call-update
  291.9 0.0 copy-done.4
  291.9 3.3 fusion.6
  295.2 3.9 %all-to-all-start.3 = ((bf16[8,128,125]{2,1,0:T(8,128)(2,1)}), bf16[8,128,125]{2,1,0:T(8,128)(2,1)S(1)}, u32[]{:S(2)}, u32[]{:S(2)}) async-start(bf16[8,128,125]{2,1,0:T(8,128)(2,1)} %bitcast.11), calls=%async_computation.4 | async-start | bytes 524288 | tf_op jit(solution)/shard_map/all_to_all | solution.py:60
  299.1 12.3 %all-to-all-done.3 = bf16[8,128,125]{2,1,0:T(8,128)(2,1)S(1)} async-done(((bf16[8,128,125]{2,1,0:T(8,128)(2,1)}), bf16[8,128,125]{2,1,0:T(8,128)(2,1)S(1)}, u32[]{:S(2)}, u32[]{:S(2)}) %all-to-all-start.3) | async-done | bytes 256032 | tf_op jit(solution)/shard_map/all_to_all | solution.py:60
  311.4 0.1 convert_reduce_fusion
  311.5 1.2 gather_fusion.1
  312.7 12.9 %all-gather.3 = bf16[8,1,128]{2,1,0:T(2,128)(2,1)S(1)} all-gather(bf16[1,1,128]{2,1,0:T(2,128)(2,1)S(1)} %convert_bitcast_fusion.1), channel_id=4, replica_groups=mesh['trow'=8,'tcol'=8,'dp'=8] {'trow'}, dimensions={0}, use_global_device_ids=true | all-gather | bytes 2304 | tf_op jit(solution)/shard_map/all_gather | solution.py:70
  325.6 11.6 %all-gather.9.cloned.1.call-done = bf16[1024,1000]{0,1:T(8,128)(2,1)} async-done(((bf16[128,1000]{0,1:T(8,128)(2,1)}), bf16[1024,1000]{0,1:T(8,128)(2,1)}) %all-gather.9.cloned.1.call-update) | async-done | bytes 2048016 | tf_op jit(solution)/shard_map/all_gather | solution.py:70
  337.2 2.2 copy.26
  339.4 0.1 dynamic-slice_convert_fusion
  339.4 0.1 copy.22
  339.5 0.7 fusion.14
  (17 shorter events, 0.2 us)
Async XLA Ops:
  8.0 1.6 copy-start
  14.7 33.2 %all-to-all-start = ((bf16[8,1024,128]{1,2,0:T(8,128)(2,1)}), bf16[8,1024,128]{1,2,0:T(8,128)(2,1)}, u32[]{:S(2)}, u32[]{:S(2)}) async-start(bf16[8,1024,128]{1,2,0:T(8,128)(2,1)} %broadcast_in_dim.20), calls=%async_computation | async-start | bytes 4194304 | tf_op jit(solution)/shard_map/all_to_all | solution.py:20
  20.8 79.7 %reduce-scatter.7.cloned.1.call-start = ((), (), s32[]{:S(2)}) async-start(), calls=%async_computation.9 | async-start | bytes 2359296 | tf_op jit(solution)/shard_map/reduce_scatter | solution.py:48
  54.9 150.9 %reduce-scatter.5.cloned.1.call-start = ((), (), s32[]{:S(2)}) async-start(), calls=%async_computation.6 | async-start | bytes 2359296 | tf_op jit(solution)/shard_map/reduce_scatter | solution.py:92
  152.6 1.3 copy-start.1
  159.2 0.8 copy-start.3
  159.2 88.1 %all-gather.7.cloned.1.call-start = ((), (), s32[]{:S(2)}) async-start(), calls=%async_computation.7 | async-start | bytes 2129920 | tf_op jit(solution)/shard_map/all_gather | solution.py:116
  160.7 176.5 %all-gather.9.cloned.1.call-start = ((), (), s32[]{:S(2)}) async-start(), calls=%async_computation.8 | async-start | bytes 2304000 | tf_op jit(solution)/shard_map/all_gather | solution.py:70
  207.0 104.5 %copy-start.2 = (f32[128,1024]{1,0:T(8,128)}, f32[128,1024]{1,0:T(8,128)S(1)}, u32[]{:S(2)}) copy-start(f32[128,1024]{1,0:T(8,128)S(1)} %get-tuple-element.3) | copy-start | bytes 1572868
  289.2 2.7 copy-start.4
  295.2 16.2 %all-to-all-start.3 = ((bf16[8,128,125]{2,1,0:T(8,128)(2,1)}), bf16[8,128,125]{2,1,0:T(8,128)(2,1)S(1)}, u32[]{:S(2)}, u32[]{:S(2)}) async-start(bf16[8,128,125]{2,1,0:T(8,128)(2,1)} %bitcast.11), calls=%async_computation.4 | async-start | bytes 524288 | tf_op jit(solution)/shard_map/all_to_all | solution.py:60
Sparse Core Ops, SparseCore 0:
  55.0 45.4 reduce-scatter.6
  159.3 46.4 reduce-scatter.4
  292.0 45.1 all-gather.8
Sparse Core Ops, SparseCore 1:
  163.6 83.6 all-gather.6
